TPU v7x, 32 devices: a whole 2x2x4 slice. The times are simulated.
32 devices in a mesh: dp: 4 (over z), sq: 8 (over y, x, core).
Axes of the slice: x: 2, y: 2, z: 4, core: 2. Of those that a mesh axis runs over, the one named last changes fastest.
Arguments:
- frames: bfloat16 [4, 1024, 1024], P('dp', 'sq'), may hold values from -6 to 6
- norm1_gain: float32 [1024], replicated, may hold values from 0.5 to 1.5
- w_qkv: bfloat16 [1024, 3072], replicated, may hold values from -0.1875 to 0.1875
- w_out: bfloat16 [1024, 1024], replicated, may hold values from -0.75 to 0.75
- norm2_gain: float32 [1024], replicated, may hold values from 0.5 to 1.5
- w_up: bfloat16 [1024, 4096], replicated, may hold values from -0.1875 to 0.1875
- w_down: bfloat16 [4096, 1024], replicated, may hold values from -0.09375 to 0.09375
- lengths: int32 [4, 8], P('dp'), may hold values from 1 to 896, as said below
- cotangent: bfloat16 [4, 1024, 1024], P('dp', 'sq'), may hold values from -6 to 6
Outputs:
- out: bfloat16 [4, 1024, 1024], P('dp', 'sq')
- d_in: float32 [4, 1024, 1024], P('dp', 'sq')
- g_norm1: float32 [1024], P('sq')
- g_qkv: float32 [1024, 3072], P('sq')
- g_out: float32 [1024, 1024], P('sq')
- g_norm2: float32 [1024], P('sq')
- g_up: float32 [1024, 4096], P('sq')
- g_down: float32 [4096, 1024], P('sq')
Inputs may be any that keep to these rules, and one draw needn't show every extreme that they name: Each row's lengths sum to 1024. In each row exactly one item has 896 frames and is neither the first nor the last item of the row; the other items share the remaining 128 frames.
All inputs are finite; a program needn't handle non-finite values.
Results may differ from a plain program's by a relative error of at most 0.025.
Values may be sent and summed in bfloat16 or wider, within the bound.
A program may use at most 256 MiB of HBM per device.

v0:
```python
import jax
import jax.numpy as jnp
from jax import lax
from jax.sharding import PartitionSpec as P

HEADS = 16
HEAD_DIM = 64
EPSILON = 1e-05
NEG_FILL = -1000000000.0
START_MAX = -1e30


def norm_scaled(values, gain):
    return values * lax.rsqrt(jnp.mean(values * values, axis=-1, keepdims=True) + EPSILON) * gain


def segment_ids(positions, item_ends):
    return jnp.sum((positions[None, :, None] >= item_ends[:, None, :]).astype(jnp.int32), axis=2)


def visible(query_pos, query_seg, key_pos, key_seg):
    return (key_pos[None, None, :] <= query_pos[None, :, None]) & (
        key_seg[:, None, :] == query_seg[:, :, None]
    )


def block_size(count, limit):
    for candidate in range(min(count, limit), 0, -1):
        if count % candidate == 0:
            return candidate
    return count


def over_blocks(carry, arrays, start, step_fn, limit):
    count = arrays[0].shape[1]
    size = block_size(count, limit)
    number = count // size
    if number == 1:
        return step_fn(carry, arrays, start)
    stacked = tuple(
        (
            jnp.swapaxes(member.reshape((member.shape[0], number, size) + member.shape[2:]), 0, 1)
            for member in arrays
        )
    )

    def turn(state, item):
        offset, pieces = item
        return (step_fn(state, pieces, start + offset * size), None)

    offsets = jnp.arange(number, dtype=jnp.int32)
    return lax.scan(turn, carry, (offsets, stacked))[0]


def contract_rows(left, right):
    return lax.dot_general(
        left, right, (((0,), (0,)), ((), ())), preferred_element_type=jnp.float32
    )


def times_transpose(left, right):
    return lax.dot_general(
        left, right, (((1,), (1,)), ((), ())), preferred_element_type=jnp.float32
    )


def heads_flat(values, batch, rows, width):
    return values.transpose(0, 2, 1, 3).reshape(batch * rows, width)


def shards(frames, norm1_gain, w_qkv, w_out, norm2_gain, w_up, w_down, lengths, cotangent):
    batch = frames.shape[0]
    rows = frames.shape[1]
    width = frames.shape[2]
    factor = HEAD_DIM ** (-0.5)
    first = lax.axis_index("sq") * rows
    query_pos = first + jnp.arange(rows, dtype=jnp.int32)
    item_ends = jnp.cumsum(lengths, axis=1)
    query_seg = segment_ids(query_pos, item_ends)
    frames_own = frames.reshape(batch * rows, width).astype(jnp.float32)
    hidden1, norm1_pull = jax.vjp(norm_scaled, frames_own, norm1_gain)
    hidden1_low = hidden1.astype(jnp.bfloat16)
    mixed = jnp.dot(hidden1_low, w_qkv, preferred_element_type=jnp.float32).astype(jnp.bfloat16)
    query_rows = mixed[:, :width].reshape(batch, rows, width)
    key_rows = mixed[:, width : 2 * width].reshape(batch, rows, width)
    value_rows = mixed[:, 2 * width :].reshape(batch, rows, width)
    queries = query_rows.reshape(batch, rows, HEADS, HEAD_DIM)
    keys_own = key_rows.reshape(batch, rows, HEADS, HEAD_DIM)
    values_own = value_rows.reshape(batch, rows, HEADS, HEAD_DIM)

    def forward_step(carry, pieces, start):
        key_piece, value_piece = pieces
        count = key_piece.shape[1]
        key_pos = start + jnp.arange(count, dtype=jnp.int32)
        key_seg = segment_ids(key_pos, item_ends)

        def forward_work(state):
            running_max, running_sum, accum = state
            keys_block = key_piece.reshape(batch, count, HEADS, HEAD_DIM)
            values_block = value_piece.reshape(batch, count, HEADS, HEAD_DIM)
            scores = (
                jnp.einsum(
                    "rqhd,rkhd->rhqk", queries, keys_block, preferred_element_type=jnp.float32
                )
                * factor
            )
            mask = visible(query_pos, query_seg, key_pos, key_seg)[:, None]
            scores = jnp.where(mask, scores, NEG_FILL)
            new_max = jnp.maximum(running_max, jnp.max(scores, axis=-1))
            weights = jnp.where(mask, jnp.exp(scores - new_max[..., None]), 0.0)
            decay = jnp.exp(running_max - new_max)
            new_sum = decay * running_sum + jnp.sum(weights, axis=-1)
            update = jnp.einsum(
                "rhqk,rkhd->rhqd",
                weights.astype(jnp.bfloat16),
                values_block,
                preferred_element_type=jnp.float32,
            )
            return (new_max, new_sum, decay[..., None] * accum + update)

        return lax.cond(start <= query_pos[-1], forward_work, lambda state: state, carry)

    start_state = (
        jnp.full((batch, HEADS, rows), START_MAX, jnp.float32),
        jnp.zeros((batch, HEADS, rows), jnp.float32),
        jnp.zeros((batch, HEADS, rows, HEAD_DIM), jnp.float32),
    )
    final_max, final_sum, accum = over_blocks(
        start_state,
        (
            lax.all_gather(key_rows, "sq", axis=1, tiled=True),
            lax.all_gather(value_rows, "sq", axis=1, tiled=True),
        ),
        jnp.int32(0),
        forward_step,
        512,
    )
    attended = heads_flat(accum / final_sum[..., None], batch, rows, width)
    log_total = final_max + jnp.log(final_sum)
    attended_low = attended.astype(jnp.bfloat16)
    middle = frames_own + jnp.dot(attended_low, w_out, preferred_element_type=jnp.float32)
    hidden2, norm2_pull = jax.vjp(norm_scaled, middle, norm2_gain)
    hidden2_low = hidden2.astype(jnp.bfloat16)
    upward = jnp.dot(hidden2_low, w_up, preferred_element_type=jnp.float32)
    active, gelu_pull = jax.vjp(jax.nn.gelu, upward)
    active_low = active.astype(jnp.bfloat16)
    result = middle + jnp.dot(active_low, w_down, preferred_element_type=jnp.float32)
    grad_top = cotangent.reshape(batch * rows, width).astype(jnp.float32)
    grad_branch = grad_top.astype(jnp.bfloat16)
    grad_down = contract_rows(active_low, grad_branch)
    grad_active = times_transpose(grad_branch, w_down)
    grad_upward = gelu_pull(grad_active)[0].astype(jnp.bfloat16)
    grad_up = contract_rows(hidden2_low, grad_upward)
    grad_hidden2 = times_transpose(grad_upward, w_up)
    grad_middle_part, grad_gain2 = norm2_pull(grad_hidden2)
    grad_middle = grad_top + grad_middle_part
    grad_attn = grad_middle.astype(jnp.bfloat16)
    grad_outproj = contract_rows(attended_low, grad_attn)
    grad_attended = times_transpose(grad_attn, w_out).astype(jnp.bfloat16)
    grad_rows_own = grad_attended.reshape(batch, rows, width)
    grad_heads = grad_attended.reshape(batch, rows, HEADS, HEAD_DIM)
    delta_rows = jnp.sum(
        (grad_attended.astype(jnp.float32) * attended).reshape(batch, rows, HEADS, HEAD_DIM), axis=3
    )
    delta = delta_rows.transpose(0, 2, 1)

    def query_step(carry, pieces, start):
        key_piece, value_piece = pieces
        count = key_piece.shape[1]
        key_pos = start + jnp.arange(count, dtype=jnp.int32)
        key_seg = segment_ids(key_pos, item_ends)

        def query_work(grad_query):
            keys_block = key_piece.reshape(batch, count, HEADS, HEAD_DIM)
            values_block = value_piece.reshape(batch, count, HEADS, HEAD_DIM)
            scores = (
                jnp.einsum(
                    "rqhd,rkhd->rhqk", queries, keys_block, preferred_element_type=jnp.float32
                )
                * factor
            )
            mask = visible(query_pos, query_seg, key_pos, key_seg)[:, None]
            shares = jnp.where(mask, jnp.exp(scores - log_total[..., None]), 0.0)
            grad_shares = jnp.einsum(
                "rqhd,rkhd->rhqk", grad_heads, values_block, preferred_element_type=jnp.float32
            )
            grad_scores = (shares * (grad_shares - delta[..., None])).astype(jnp.bfloat16)
            return grad_query + jnp.einsum(
                "rhqk,rkhd->rhqd", grad_scores, keys_block, preferred_element_type=jnp.float32
            )

        return lax.cond(start <= query_pos[-1], query_work, lambda state: state, carry)

    zero_query = jnp.zeros((batch, HEADS, rows, HEAD_DIM), jnp.float32)
    grad_query = over_blocks(
        zero_query,
        (
            lax.all_gather(key_rows, "sq", axis=1, tiled=True),
            lax.all_gather(value_rows, "sq", axis=1, tiled=True),
        ),
        jnp.int32(0),
        query_step,
        512,
    )

    def key_step(carry, pieces, start):
        query_piece, grad_piece, total_piece, delta_piece = pieces
        count = query_piece.shape[1]
        remote_pos = start + jnp.arange(count, dtype=jnp.int32)
        remote_seg = segment_ids(remote_pos, item_ends)

        def key_work(state):
            grad_key, grad_value = state
            remote_queries = query_piece.reshape(batch, count, HEADS, HEAD_DIM)
            remote_grads = grad_piece.reshape(batch, count, HEADS, HEAD_DIM)
            scores = (
                jnp.einsum(
                    "rqhd,rkhd->rhqk", remote_queries, keys_own, preferred_element_type=jnp.float32
                )
                * factor
            )
            mask = visible(remote_pos, remote_seg, query_pos, query_seg)[:, None]
            shares = jnp.where(
                mask, jnp.exp(scores - total_piece.transpose(0, 2, 1)[..., None]), 0.0
            )
            grad_value = grad_value + jnp.einsum(
                "rhqk,rqhd->rhkd",
                shares.astype(jnp.bfloat16),
                remote_grads,
                preferred_element_type=jnp.float32,
            )
            grad_shares = jnp.einsum(
                "rqhd,rkhd->rhqk", remote_grads, values_own, preferred_element_type=jnp.float32
            )
            grad_scores = (
                shares * (grad_shares - delta_piece.transpose(0, 2, 1)[..., None])
            ).astype(jnp.bfloat16)
            grad_key = grad_key + jnp.einsum(
                "rhqk,rqhd->rhkd", grad_scores, remote_queries, preferred_element_type=jnp.float32
            )
            return (grad_key, grad_value)

        return lax.cond(start + count - 1 >= first, key_work, lambda state: state, carry)

    grad_key, grad_value = over_blocks(
        (zero_query, zero_query),
        (
            lax.all_gather(query_rows, "sq", axis=1, tiled=True),
            lax.all_gather(grad_rows_own, "sq", axis=1, tiled=True),
            lax.all_gather(
                log_total.transpose(0, 2, 1).astype(jnp.bfloat16), "sq", axis=1, tiled=True
            ).astype(jnp.float32),
            lax.all_gather(delta_rows.astype(jnp.bfloat16), "sq", axis=1, tiled=True).astype(
                jnp.float32
            ),
        ),
        jnp.int32(0),
        key_step,
        512,
    )
    grad_mixed = jnp.concatenate(
        [
            heads_flat(grad_query * factor, batch, rows, width),
            heads_flat(grad_key * factor, batch, rows, width),
            heads_flat(grad_value, batch, rows, width),
        ],
        axis=1,
    ).astype(jnp.bfloat16)
    grad_qkv = contract_rows(hidden1_low, grad_mixed)
    grad_hidden1 = times_transpose(grad_mixed, w_qkv)
    grad_frames_part, grad_gain1 = norm1_pull(grad_hidden1)
    grad_frames = (grad_middle + grad_frames_part).reshape(batch, rows, width)
    result_rows = result.astype(jnp.bfloat16).reshape(batch, rows, width)
    shares_sq = (
        lax.psum_scatter(grad_gain1, "sq", scatter_dimension=0, tiled=True),
        lax.psum_scatter(grad_qkv, "sq", scatter_dimension=0, tiled=True),
        lax.psum_scatter(grad_outproj, "sq", scatter_dimension=0, tiled=True),
        lax.psum_scatter(grad_gain2, "sq", scatter_dimension=0, tiled=True),
        lax.psum_scatter(grad_up, "sq", scatter_dimension=0, tiled=True),
        lax.psum_scatter(grad_down, "sq", scatter_dimension=0, tiled=True),
    )
    totals = (
        lax.psum(shares_sq[0].astype(jnp.bfloat16), "dp").astype(jnp.float32),
        lax.psum(shares_sq[1].astype(jnp.bfloat16), "dp").astype(jnp.float32),
        lax.psum(shares_sq[2].astype(jnp.bfloat16), "dp").astype(jnp.float32),
        lax.psum(shares_sq[3].astype(jnp.bfloat16), "dp").astype(jnp.float32),
        lax.psum(shares_sq[4].astype(jnp.bfloat16), "dp").astype(jnp.float32),
        lax.psum(shares_sq[5].astype(jnp.bfloat16), "dp").astype(jnp.float32),
    )
    return (
        result_rows,
        grad_frames,
        totals[0],
        totals[1],
        totals[2],
        totals[3],
        totals[4],
        totals[5],
    )


def solution(mesh):
    return jax.shard_map(
        shards,
        mesh=mesh,
        in_specs=(
            P("dp", "sq", None),
            P(),
            P(),
            P(),
            P(),
            P(),
            P(),
            P("dp", None),
            P("dp", "sq", None),
        ),
        out_specs=(
            P("dp", "sq", None),
            P("dp", "sq", None),
            P("sq"),
            P("sq", None),
            P("sq", None),
            P("sq"),
            P("sq", None),
            P("sq", None),
        ),
        check_vma=False,
    )
```

profile of v0, /device:TPU:0, one launch (start us, length us, event | category | flops | bytes accessed | tf_op | source)
XLA Modules:
  0.0 698.9 jit_solution(101815978232163255)
XLA Ops:
  18.7 26.0 %all-gather.9.cloned.1.call-done = bf16[1024,1024]{1,0:T(8,128)(2,1)} async-done(((bf16[128,1024]{1,0:T(8,128)(2,1)}), bf16[1024,1024]{1,0:T(8,128)(2,1)}) %all-gather.9.cloned.1.call-update) | async-done | bytes 2097168 | tf_op jit(solution)/shard_map/all_gather | solution.py:131
  48.6 26.5 %all-gather.11.cloned.1.call-done = bf16[1024,1024]{1,0:T(8,128)(2,1)} async-done(((bf16[128,1024]{1,0:T(8,128)(2,1)}), bf16[1024,1024]{1,0:T(8,128)(2,1)}) %all-gather.11.cloned.1.call-update) | async-done | bytes 2097168 | tf_op jit(solution)/shard_map/all_gather | solution.py:132
  79.1 13.9 %while.45 = (s32[]{:T(128)}, f32[1,16,128]{2,1,0:T(8,128)S(1)}, f32[1,16,128]{2,1,0:T(8,128)S(1)}, f32[1,16,128,64]{2,3,1,0:T(8,128)S(1)}, s32[2]{0:T(128)S(1)},...) while((s32[]{:T(128)}, f32[1,16,128]{2,1,0:T(8,128)S(1)}, ...), condition=%wide.region_9.10_spmd, body=%wide.region_3.9_spmd.sunk | while | flops 282544640 | bytes 20628860 | solution.py:52
  83.0 6.1 conditional.8
  103.2 7.7 %fusion.60 = bf16[128,4096]{1,0:T(8,128)(2,1)S(1)} fusion(f32[128,4096]{1,0:T(8,128)S(1)} %fusion.92, bf16[4096,1024]{1,0:T(8,128)(2,1)} %param.27, bf16[1,128,1024]{2,1,0:T(8,128)(2,1)S(1)} %copy-done.18), kind=kOutput, calls=%fused_computation.80 | convolution fusion | flops 1084227584 | bytes 11796480 | tf_op jit(solution)/shard_map/dot_general | solution.py:62
  129.7 15.0 %all_gather.25 = bf16[1,1024,16]{1,2,0:T(8,128)(2,1)S(1)} all-gather(bf16[1,128,16]{1,2,0:T(8,128)(2,1)S(1)} %bitcast_convert_fusion), channel_id=1, replica_groups=mesh['dp'=4,'sq'=8] {'sq'}, dimensions={1}, use_global_device_ids=true | all-gather | bytes 36864 | tf_op jit(solution)/shard_map/all_gather | solution.py:253
  145.3 8.0 %all_gather.23 = bf16[1,1024,16]{1,2,0:T(8,128)(2,1)S(1)} all-gather(bf16[1,128,16]{1,2,0:T(8,128)(2,1)S(1)} %get-tuple-element.1073), channel_id=1, replica_groups=mesh['dp'=4,'sq'=8] {'sq'}, dimensions={1}, use_global_device_ids=true | all-gather | bytes 36864 | tf_op jit(solution)/shard_map/all_gather | solution.py:250
  155.3 20.4 %while.46 = (s32[]{:T(128)}, f32[1,16,128,64]{2,3,1,0:T(8,128)}, s32[2]{0:T(128)}, s32[128]{0:T(128)}, s32[1,8]{1,0:T(1,128)}, /*index=5*/s32[1,128]{1,0:T(1,128...) while((s32[]{:T(128)}, f32[1,16,128,64]{2,3,1,0:T(8,128)}, ...), condition=%wide.region_17.18_spmd, body=%wide.region_13.17_spmd.sunk | while | flops 409285120 | bytes 17499484 | solution.py:52
  159.7 11.6 %conditional.9 = (f32[1,16,128,64]{2,3,1,0:T(8,128)}) conditional(s32[]{:T(128)} %convert_element_type.291, f32[1,16,128,64]{2,3,1,0:T(8,128)} %get-tuple-element.1437, (s32[]{:T(128)}, s32[512]{0:T(512)S(1)}, s32[128]{0:T(128)}, s32[1,512,8]{1,2,0:T(8,128)S(1)}, s32[1,128]{1,0:T(1,128)}, /*index=5*/bf16[2,1,512,1024]{2,3,1,0:T(8,128)(2,1)}, ...), branch_computations={%region_14.14_spmd, %region_15.16_spmd} | conditional | flops 409276416 | bytes 17476628 | solution.py:192
  182.4 36.2 %while.47 = (s32[]{:T(128)}, f32[1,16,128,64]{2,3,1,0:T(8,128)S(1)}, f32[1,16,128,64]{2,3,1,0:T(8,128)}, s32[2]{0:T(128)S(1)}, s32[]{:T(128)}, /*index=5*/s32[1,...) while((s32[]{:T(128)}, ...), condition=%wide.region_22.23_spmd.clone.clone, body=%wide.region_18.22_spmd.clone.clone.sunk | while | flops 547828352 | bytes 28265440 | solution.py:52
  184.5 16.3 %conditional.10 = ((f32[1,16,128,64]{2,3,1,0:T(8,128)S(1)}, f32[1,16,128,64]{2,3,1,0:T(8,128)})) conditional(s32[]{:T(128)} %convert_element_type.293, (f32[1,16,128,64]{2,3,1,0:T(8,128)S(1)}, f32[1,16,128,64]{2,3,1,0:T(8,128)}) %tuple.150, (s32[]{:T(128)}, s32[]{:T(128)}, s32[512]{0:T(512)S(1)}, s32[1,128]{1,0:T(1,128)S(1)}, ...), branch_computations={%region_19.19_spmd, %region_20.21_spmd} | conditional | flops 547819648 | bytes 28242020 | solution.py:243
  190.0 6.2 fusion.42
  202.8 15.9 %conditional.10 = ((f32[1,16,128,64]{2,3,1,0:T(8,128)S(1)}, f32[1,16,128,64]{2,3,1,0:T(8,128)})) conditional(s32[]{:T(128)} %convert_element_type.293, (f32[1,16,128,64]{2,3,1,0:T(8,128)S(1)}, f32[1,16,128,64]{2,3,1,0:T(8,128)}) %tuple.150, (s32[]{:T(128)}, s32[]{:T(128)}, s32[512]{0:T(512)S(1)}, s32[1,128]{1,0:T(1,128)S(1)}, ...), branch_computations={%region_19.19_spmd, %region_20.21_spmd} | conditional | flops 547819648 | bytes 28242020 | solution.py:243
  208.3 6.2 fusion.42
  219.8 7.5 %fusion.72 = f32[1024,3072]{1,0:T(8,128)} fusion(bf16[128,1024]{0,1:T(8,128)(2,1)S(1)} %bitcast.228, bf16[128,1024]{0,1:T(8,128)(2,1)S(1)} %bitcast.230, bf16[128,1024]{0,1:T(8,128)(2,1)} %bitcast.226, bf16[1,128,1024]{2,1,0:T(8,128)(2,1)S(1)} %copy-done.4, f32[1024]{0:T(1024)S(1)} %copy-done.30, f32[128]{0:T(128)S(1)} %copy-done.38), kind=kOutput, calls=%fused_computation.111 | convolution fusion | flops 808189952 | bytes 13636096 | tf_op jit(solution)/shard_map/dot_general | solution.py:56
  228.5 11.2 %fusion.91 = f32[1024,4096]{1,0:T(8,128)} fusion(bf16[128,4096]{1,0:T(8,128)(2,1)S(1)} %copy-done.9, f32[128,1024]{1,0:T(8,128)S(1)} %get-tuple-element.1089, f32[1024]{0:T(1024)S(1)} %copy-done.29, f32[128]{0:T(128)S(1)} %copy-done.35), kind=kOutput, calls=%fused_computation.140 | convolution fusion | flops 1074135040 | bytes 18354688 | tf_op jit(solution)/shard_map/dot_general | solution.py:56
  241.9 8.9 %fusion.74 = f32[4096,1024]{1,0:T(8,128)} fusion(bf16[1,128,1024]{2,1,0:T(8,128)(2,1)S(1)} %copy-done.19, f32[128,4096]{1,0:T(8,128)S(1)} %copy-done.3), kind=kOutput, calls=%fused_computation.113 | convolution fusion | flops 1078460416 | bytes 19136512 | tf_op jit(solution)/shard_map/dot_general | solution.py:56
  252.8 67.5 %reduce-scatter.5.cloned.1.call-done = f32[128,3072]{1,0:T(8,128)} async-done(((f32[1024,3072]{1,0:T(8,128)}), f32[128,3072]{1,0:T(8,128)}) %reduce-scatter.5.cloned.1.call-update) | async-done | bytes 1572880 | tf_op jit(solution)/shard_map/reduce_scatter | solution.py:276
  322.6 117.6 %reduce-scatter.9.cloned.1.call-done = f32[128,4096]{1,0:T(8,128)} async-done(((f32[1024,4096]{1,0:T(8,128)}), f32[128,4096]{1,0:T(8,128)}) %reduce-scatter.9.cloned.1.call-update) | async-done | bytes 2097168 | tf_op jit(solution)/shard_map/reduce_scatter | solution.py:279
  442.9 117.3 %reduce-scatter.11.cloned.1.call-done = f32[512,1024]{1,0:T(8,128)} async-done(((f32[4096,1024]{1,0:T(8,128)}), f32[512,1024]{1,0:T(8,128)}) %reduce-scatter.11.cloned.1.call-update) | async-done | bytes 2097168 | tf_op jit(solution)/shard_map/reduce_scatter | solution.py:280
  564.8 5.7 fusion.62
  575.8 13.8 %all-reduce.2 = (bf16[1024]{0:T(1024)(128)(2,1)S(1)}, bf16[1024]{0:T(1024)(128)(2,1)S(1)}) all-reduce(f32[1024]{0:T(1024)S(1)} %get-tuple-element.989, f32[1024]{0:T(1024)S(1)} %copy-done.36), channel_id=6, replica_groups=mesh['dp'=4,'sq'=8] {'sq'}, use_global_device_ids=true, to_apply=%region_25.26.clone | all-reduce | flops 2048 | bytes 12288
  589.8 12.4 %all-reduce.3 = (bf16[128]{0:T(256)(128)(2,1)S(1)}, bf16[128]{0:T(256)(128)(2,1)S(1)}) all-reduce(bf16[128]{0:T(256)(128)(2,1)S(1)} %dynamic-slice.7, bf16[128]{0:T(256)(128)(2,1)S(1)} %dynamic-slice.6), channel_id=1, replica_groups=mesh['dp'=4,'sq'=8] {'dp'}, use_global_device_ids=true, to_apply=%region_26.27 | all-reduce | flops 256 | bytes 1024 | tf_op jit(solution)/shard_map/psum | solution.py:283
  604.2 81.7 %all-reduce.7.cloned.1.call-done = (bf16[128,3072]{1,0:T(8,128)(2,1)}, bf16[128,1024]{1,0:T(8,128)(2,1)}, bf16[128,4096]{1,0:T(8,128)(2,1)}, bf16[512,1024]{1,0:T(8,128)(2,1)}) async-done(((bf16[128,3072]{1,0:T(8,128)(2,1)}, bf16[128,1024]{1,0:T(8,128)(2,1)}, bf16[128,4096]{1,0:T(8,128)(2,1)}, bf16[512,1024]{1,0:T(8,128)(2,1)}), (bf16[128,3072]{1,0:T(8,128)(2,1)}, bf16[128,1024]{1,0:T(8,128)(2,1)}, ...) | async-done | bytes 3145744 | tf_op jit(solution)/shard_map/psum | solution.py:284
  (242 shorter events, 138.3 us)
Async XLA Ops:
  7.2 89.5 %copy-start = (bf16[1024,1024]{1,0:T(8,128)(2,1)S(1)}, bf16[1024,1024]{1,0:T(8,128)(2,1)}, u32[]{:S(2)}) copy-start(bf16[1024,1024]{1,0:T(8,128)(2,1)} %param.24) | copy-start | bytes 6291460
  7.2 37.5 %all-gather.9.cloned.1.call-start = ((), (), s32[]{:S(2)}) async-start(), calls=%async_computation.8 | async-start | bytes 2359296 | tf_op jit(solution)/shard_map/all_gather | solution.py:131
  14.0 61.1 %all-gather.11.cloned.1.call-start = ((), (), s32[]{:S(2)}) async-start(), calls=%async_computation.9 | async-start | bytes 2359296 | tf_op jit(solution)/shard_map/all_gather | solution.py:132
  14.7 109.4 %all-gather.13.cloned.1.call-start = ((), (), s32[]{:S(2)}) async-start(), calls=%async_computation.10 | async-start | bytes 2359296 | tf_op jit(solution)/shard_map/all_gather | solution.py:248
  15.4 162.1 %all-gather.15.cloned.1.call-start = ((), (), s32[]{:S(2)}) async-start(), calls=%async_computation.11 | async-start | bytes 2359296 | tf_op jit(solution)/shard_map/all_gather | solution.py:249
  98.2 16.3 %copy-start.34 = (f32[128]{0:T(128)}, f32[128]{0:T(128)S(1)}, u32[]{:S(2)}) copy-start(f32[128]{0:T(128)S(1)} %fusion.88) | copy-start | bytes 1540
  98.3 12.7 %slice-start = ((s8[8388608]{0:T(1024)(128)(4,1)}), s8[4194304]{0:T(1024)(128)(4,1)S(1)}, s32[]{:S(2)}) async-start(s8[8388608]{0:T(1024)(128)(4,1)} %bitcast.209), calls=%async_computation.13 | async-start | bytes 8388608
  103.2 7.8 %copy-start.2 = (f32[128,4096]{1,0:T(8,128)}, f32[128,4096]{1,0:T(8,128)S(1)}, u32[]{:S(2)}) copy-start(f32[128,4096]{1,0:T(8,128)S(1)} %fusion.92) | copy-start | bytes 6291460
  103.2 7.8 %slice-start.1 = ((s8[8388608]{0:T(1024)(128)(4,1)}), s8[4194304]{0:T(1024)(128)(4,1)S(1)}, s32[]{:S(2)}) async-start(s8[8388608]{0:T(1024)(128)(4,1)} %bitcast.209), calls=%async_computation.14 | async-start | bytes 8388608
  117.3 133.6 %reduce-scatter.7.cloned.1.call-start = ((), (), s32[]{:S(2)}) async-start(), calls=%async_computation.5 | async-start | bytes 4718592 | tf_op jit(solution)/shard_map/reduce_scatter | solution.py:277
  121.3 198.9 %reduce-scatter.5.cloned.1.call-start = ((), (), s32[]{:S(2)}) async-start(), calls=%async_computation.4 | async-start | bytes 14155776 | tf_op jit(solution)/shard_map/reduce_scatter | solution.py:276
  182.4 37.4 %copy-start.30 = (f32[1024]{0:T(1024)S(1)}, f32[1024]{0:T(1024)}, u32[]{:S(2)}) copy-start(f32[1024]{0:T(1024)} %param.22) | copy-start | bytes 12292
  182.4 37.4 %copy-start.38 = (f32[128]{0:T(128)S(1)}, f32[128]{0:T(128)}, u32[]{:S(2)}) copy-start(f32[128]{0:T(128)} %copy-done.37) | copy-start | bytes 1540
  219.7 7.6 %copy-start.23 = (bf16[1,16,128,64]{2,3,1,0:T(8,128)(2,1)}, bf16[1,16,128,64]{2,3,1,0:T(8,128)(2,1)S(1)}, u32[]{:S(2)}) copy-start(bf16[1,16,128,64]{2,3,1,0:T(8,128)(2,1)S(1)} %convert.20) | copy-start | bytes 786436
  219.8 7.5 %copy-start.25 = (bf16[1,16,128,64]{2,3,1,0:T(8,128)(2,1)}, bf16[1,16,128,64]{2,3,1,0:T(8,128)(2,1)S(1)}, u32[]{:S(2)}) copy-start(bf16[1,16,128,64]{2,3,1,0:T(8,128)(2,1)S(1)} %multiply_convert_fusion.2) | copy-start | bytes 786436
  227.3 212.8 %reduce-scatter.9.cloned.1.call-start = ((), (), s32[]{:S(2)}) async-start(), calls=%async_computation.6 | async-start | bytes 18874368 | tf_op jit(solution)/shard_map/reduce_scatter | solution.py:279
  239.7 320.4 %reduce-scatter.11.cloned.1.call-start = ((), (), s32[]{:S(2)}) async-start(), calls=%async_computation.7 | async-start | bytes 18874368 | tf_op jit(solution)/shard_map/reduce_scatter | solution.py:280
  250.9 435.0 %all-reduce.7.cloned.1.call-start = ((), (), s32[]{:S(2)}) async-start(), calls=%async_computation.12 | async-start | bytes 6291456 | tf_op jit(solution)/shard_map/psum | solution.py:284
  564.8 5.8 copy-start.22
  564.8 5.8 copy-start.24
  564.8 5.8 copy-start.26
  564.8 5.8 copy-start.39
  570.6 32.6 %copy-start.41 = (f32[128]{0:T(128)S(1)}, f32[128]{0:T(128)}, u32[]{:S(2)}) copy-start(f32[128]{0:T(128)} %copy-done.40) | copy-start | bytes 1540
  570.6 32.6 %copy-start.6 = (f32[128,1024]{1,0:T(8,128)S(1)}, f32[128,1024]{1,0:T(8,128)}, u32[]{:S(2)}) copy-start(f32[128,1024]{1,0:T(8,128)} %copy-done.5) | copy-start | bytes 1572868
  (33 other events, 85.8 us)
Sparse Core Ops, SparseCore 0:
  14.1 30.5 all-gather.8
  47.2 27.8 all-gather.10
  77.0 27.8 all-gather.12
  117.5 34.1 all-gather.14
  154.8 51.3 reduce-scatter.6
  227.5 92.7 reduce-scatter.4
  324.2 115.9 reduce-scatter.8
  444.2 115.9 reduce-scatter.10
  563.5 122.3 all-reduce.6
where the time goes:
time: 700 us; the launch traced here: 699 us
  waiting for transfers between devices  438 us (63%)
  matrix products  103 us (15%)
  local copies, waits for them, and re-layouts  50.6 us (7%)
  blocking collectives  49.2 us (7%)
  other arithmetic  35.8 us (5%)
  between operations  15 us (2%)
    reduce_scatter x1, waiting for transfers between devices, shards(): lax.psum_scatter(grad_up, 'sq', scatter_dimension=0, tiled=True)  118 us
    reduce_scatter x1, waiting for transfers between devices, shards(): lax.psum_scatter(grad_down, 'sq', scatter_dimension=0, tiled=True)  117 us
    psum x1, waiting for transfers between devices, shards(): lax.psum(shares_sq[1].astype(jnp.bfloat16), 'dp').astype(jnp.float32)  81.7 us
    reduce_scatter x1, waiting for transfers between devices, shards(): lax.psum_scatter(grad_qkv, 'sq', scatter_dimension=0, tiled=True)  67.5 us
    dot_general x4, matrix products, contract_rows(): lax.dot_general(left, right, (((0,), (0,)), ((), ())), preferred_element_...  31.4 us
    all_gather x1, waiting for transfers between devices, shards(): lax.all_gather(value_rows, 'sq', axis=1, tiled=True)  26.5 us
    all_gather x1, waiting for transfers between devices, shards(): lax.all_gather(key_rows, 'sq', axis=1, tiled=True)  26 us
    dot_general x4, matrix products, times_transpose(): lax.dot_general(left, right, (((1,), (1,)), ((), ())), preferred_element_...  18.2 us
  transfers between devices with their start and end apart: 9, of which 6 were waited for; matrix products, arithmetic and copies ran while one was open for 24% of the time, Pallas kernels for 0%

commit v1 on v0

--- a/solution.py
+++ b/solution.py
@@ -125,12 +125,30 @@
         jnp.zeros((batch, HEADS, rows), jnp.float32),
         jnp.zeros((batch, HEADS, rows, HEAD_DIM), jnp.float32),
     )
+
+    def make_the_seats_all(z):
+        long_array, answer, low = (lax.axis_size("sq"), lax.axis_index("sq"), z.shape[1])
+        log = [(no, (no + 1) % long_array) for no in range(long_array)]
+        table = [(no, (no - 1) % long_array) for no in range(long_array)]
+        upper = jnp.zeros((*z.shape[:1], long_array * low, *z.shape[2:]), z.dtype)
+        upper = lax.dynamic_update_slice_in_dim(upper, z, answer * low, axis=1)
+        view_out = ready = z
+        val2 = long_array // 2
+        for dev_j in range(1, val2 + 1):
+            view_out = lax.ppermute(view_out, "sq", log)
+            upper = lax.dynamic_update_slice_in_dim(
+                upper, view_out, (answer - dev_j) % long_array * low, axis=1
+            )
+            if dev_j < long_array - val2:
+                ready = lax.ppermute(ready, "sq", table)
+                upper = lax.dynamic_update_slice_in_dim(
+                    upper, ready, (answer + dev_j) % long_array * low, axis=1
+                )
+        return upper
+
     final_max, final_sum, accum = over_blocks(
         start_state,
-        (
-            lax.all_gather(key_rows, "sq", axis=1, tiled=True),
-            lax.all_gather(value_rows, "sq", axis=1, tiled=True),
-        ),
+        (lax.all_gather(key_rows, "sq", axis=1, tiled=True), make_the_seats_all(value_rows)),
         jnp.int32(0),
         forward_step,
         512,

time: 700 us -> 692 us (0.989)
  waiting for transfers between devices: 438 us -> 400 us
  local copies, waits for them, and re-layouts: 50.6 us -> 63.8 us
  starting transfers between devices: 0.63 us -> 9.32 us
    all_gather x1, waiting for transfers between devices: 26.5 us -> 0.01 us  [shards(): lax.all_gather(value_rows, 'sq', axis=1, tiled=True)]
    all_gather x1, waiting for transfers between devices: 26 us -> 0.01 us  [shards(): lax.all_gather(key_rows, 'sq', axis=1, tiled=True)]
    ppermute x0 -> x7, waiting for transfers between devices: none -> 15 us  [the longest x4 8.78 us: make_the_seats_all(): view_out = lax.ppermute(view_out, 'sq', log)]
    ppermute x0 -> x7, starting transfers between devices: none -> 8.74 us  [the longest x3 7.74 us: make_the_seats_all(): ready = lax.ppermute(ready, 'sq', table)]
    dynamic_update_slice x0 -> x8, local copies, waits for them, and re-layouts: none -> 8.6 us  [the longest x4 4.78 us: make_the_seats_all(): lax.dynamic_update_slice_in_dim(upper, view_out, (answer - dev_j) % long_...]
    unnamed x94 -> x92, local copies, waits for them, and re-layouts: 17.1 us -> 17 us
  transfers between devices with their start and end apart: 9 -> 16, of which waited for: 6 -> 8; matrix products, arithmetic and copies ran while one was open for 24% -> 26% of each run, Pallas kernels for 0% -> 0%
where the time goes in v1:
time: 692 us; the launch traced here: 685 us
  waiting for transfers between devices  400 us (58%)
  matrix products  103 us (15%)
  local copies, waits for them, and re-layouts  63.8 us (9%)
  blocking collectives  49.6 us (7%)
  other arithmetic  37.3 us (5%)
  between operations  15.3 us (2%)
  starting transfers between devices  9.32 us (1%)
    reduce_scatter x1, waiting for transfers between devices, shards(): lax.psum_scatter(grad_up, 'sq', scatter_dimension=0, tiled=True)  118 us
    reduce_scatter x1, waiting for transfers between devices, shards(): lax.psum_scatter(grad_down, 'sq', scatter_dimension=0, tiled=True)  117 us
    psum x1, waiting for transfers between devices, shards(): lax.psum(shares_sq[1].astype(jnp.bfloat16), 'dp').astype(jnp.float32)  81.7 us
    reduce_scatter x1, waiting for transfers between devices, shards(): lax.psum_scatter(grad_qkv, 'sq', scatter_dimension=0, tiled=True)  67.4 us
    dot_general x4, matrix products, contract_rows(): lax.dot_general(left, right, (((0,), (0,)), ((), ())), preferred_element_...  31.5 us
    dot_general x4, matrix products, times_transpose(): lax.dot_general(left, right, (((1,), (1,)), ((), ())), preferred_element_...  18.2 us
    unnamed x92, local copies, waits for them, and re-layouts  17 us
    all_gather x1, blocking collectives, shards(): lax.all_gather(delta_rows.astype(jnp.bfloat16), 'sq', axis=1, tiled=True)  15.2 us
  transfers between devices with their start and end apart: 16, of which 8 were waited for; matrix products, arithmetic and copies ran while one was open for 26% of the time, Pallas kernels for 0%

profile of v1, /device:TPU:0, one launch (start us, length us, event | category | flops | bytes accessed | tf_op | source)
XLA Modules:
  0.0 684.9 jit_solution(7976593075149619330)
XLA Ops:
  41.4 6.2 collective-permute-done.5
  59.6 14.3 %while.45 = (s32[]{:T(128)}, f32[1,16,128]{2,1,0:T(8,128)S(1)}, f32[1,16,128]{2,1,0:T(8,128)S(1)}, f32[1,16,128,64]{2,3,1,0:T(8,128)S(1)}, s32[2]{0:T(128)S(1)},...) while((s32[]{:T(128)}, f32[1,16,128]{2,1,0:T(8,128)S(1)}, ...), condition=%wide.region_9.10_spmd, body=%wide.region_3.9_spmd.sunk | while | flops 282544640 | bytes 20628860 | solution.py:52
  63.4 6.1 conditional.8
  84.1 7.7 %fusion.60 = bf16[128,4096]{1,0:T(8,128)(2,1)S(1)} fusion(f32[128,4096]{1,0:T(8,128)S(1)} %fusion.92, bf16[4096,1024]{1,0:T(8,128)(2,1)} %param.27, bf16[1,128,1024]{2,1,0:T(8,128)(2,1)S(1)} %copy-done.19), kind=kOutput, calls=%fused_computation.80 | convolution fusion | flops 1084227584 | bytes 11796480 | tf_op jit(solution)/shard_map/dot_general | solution.py:62
  110.6 15.2 %all_gather.24 = bf16[1,1024,16]{1,2,0:T(8,128)(2,1)S(1)} all-gather(bf16[1,128,16]{1,2,0:T(8,128)(2,1)S(1)} %bitcast_convert_fusion), channel_id=1, replica_groups=mesh['dp'=4,'sq'=8] {'sq'}, dimensions={1}, use_global_device_ids=true | all-gather | bytes 36864 | tf_op jit(solution)/shard_map/all_gather | solution.py:271
  126.4 8.1 %all_gather.22 = bf16[1,1024,16]{1,2,0:T(8,128)(2,1)S(1)} all-gather(bf16[1,128,16]{1,2,0:T(8,128)(2,1)S(1)} %get-tuple-element.1073), channel_id=1, replica_groups=mesh['dp'=4,'sq'=8] {'sq'}, dimensions={1}, use_global_device_ids=true | all-gather | bytes 36864 | tf_op jit(solution)/shard_map/all_gather | solution.py:268
  140.7 20.1 %while.46 = (s32[]{:T(128)}, f32[1,16,128,64]{2,3,1,0:T(8,128)}, s32[2]{0:T(128)}, s32[128]{0:T(128)}, s32[1,8]{1,0:T(1,128)}, /*index=5*/s32[1,128]{1,0:T(1,128...) while((s32[]{:T(128)}, f32[1,16,128,64]{2,3,1,0:T(8,128)}, ...), condition=%wide.region_17.18_spmd, body=%wide.region_13.17_spmd.sunk | while | flops 409285120 | bytes 17499484 | solution.py:52
  145.0 11.5 %conditional.9 = (f32[1,16,128,64]{2,3,1,0:T(8,128)}) conditional(s32[]{:T(128)} %convert_element_type.291, f32[1,16,128,64]{2,3,1,0:T(8,128)} %get-tuple-element.1438, (s32[]{:T(128)}, s32[512]{0:T(512)S(1)}, s32[128]{0:T(128)}, s32[1,512,8]{1,2,0:T(8,128)S(1)}, s32[1,128]{1,0:T(1,128)}, /*index=5*/bf16[2,1,512,1024]{2,3,1,0:T(8,128)(2,1)}, ...), branch_computations={%region_14.14_spmd, %region_15.16_spmd} | conditional | flops 409276416 | bytes 17476628 | solution.py:210
  150.9 5.6 fusion.23
  167.5 37.0 %while.47 = (s32[]{:T(128)}, f32[1,16,128,64]{2,3,1,0:T(8,128)S(1)}, f32[1,16,128,64]{2,3,1,0:T(8,128)}, s32[2]{0:T(128)S(1)}, s32[]{:T(128)}, /*index=5*/s32[1,...) while((s32[]{:T(128)}, ...), condition=%wide.region_22.23_spmd.clone.clone, body=%wide.region_18.22_spmd.clone.clone.sunk | while | flops 547828352 | bytes 28265440 | solution.py:52
  169.5 16.5 %conditional.10 = ((f32[1,16,128,64]{2,3,1,0:T(8,128)S(1)}, f32[1,16,128,64]{2,3,1,0:T(8,128)})) conditional(s32[]{:T(128)} %convert_element_type.293, (f32[1,16,128,64]{2,3,1,0:T(8,128)S(1)}, f32[1,16,128,64]{2,3,1,0:T(8,128)}) %tuple.151, (s32[]{:T(128)}, s32[]{:T(128)}, s32[512]{0:T(512)S(1)}, s32[1,128]{1,0:T(1,128)}, ...), branch_computations={%region_19.19_spmd, %region_20.21_spmd} | conditional | flops 547819648 | bytes 28242020 | solution.py:261
  175.6 6.2 fusion.42
  187.9 16.6 %conditional.10 = ((f32[1,16,128,64]{2,3,1,0:T(8,128)S(1)}, f32[1,16,128,64]{2,3,1,0:T(8,128)})) conditional(s32[]{:T(128)} %convert_element_type.293, (f32[1,16,128,64]{2,3,1,0:T(8,128)S(1)}, f32[1,16,128,64]{2,3,1,0:T(8,128)}) %tuple.151, (s32[]{:T(128)}, s32[]{:T(128)}, s32[512]{0:T(512)S(1)}, s32[1,128]{1,0:T(1,128)}, ...), branch_computations={%region_19.19_spmd, %region_20.21_spmd} | conditional | flops 547819648 | bytes 28242020 | solution.py:261
  194.1 6.2 fusion.42
  205.7 7.5 %fusion.72 = f32[1024,3072]{1,0:T(8,128)} fusion(bf16[128,1024]{0,1:T(8,128)(2,1)S(1)} %bitcast.232, bf16[128,1024]{0,1:T(8,128)(2,1)S(1)} %bitcast.234, bf16[128,1024]{0,1:T(8,128)(2,1)} %bitcast.230, bf16[1,128,1024]{2,1,0:T(8,128)(2,1)S(1)} %copy-done.4, f32[1024]{0:T(1024)S(1)} %copy-done.31, f32[128]{0:T(128)S(1)} %copy-done.37), kind=kOutput, calls=%fused_computation.111 | convolution fusion | flops 808189952 | bytes 13636096 | tf_op jit(solution)/shard_map/dot_general | solution.py:56
  214.4 11.3 %fusion.91 = f32[1024,4096]{1,0:T(8,128)} fusion(bf16[128,4096]{1,0:T(8,128)(2,1)S(1)} %copy-done.9, f32[128,1024]{1,0:T(8,128)S(1)} %get-tuple-element.1090, f32[1024]{0:T(1024)S(1)} %copy-done.30, f32[128]{0:T(128)S(1)} %copy-done.34), kind=kOutput, calls=%fused_computation.148 | convolution fusion | flops 1074135040 | bytes 18354688 | tf_op jit(solution)/shard_map/dot_general | solution.py:56
  227.9 8.8 %fusion.74 = f32[4096,1024]{1,0:T(8,128)} fusion(bf16[1,128,1024]{2,1,0:T(8,128)(2,1)S(1)} %copy-done.20, f32[128,4096]{1,0:T(8,128)S(1)} %copy-done.3), kind=kOutput, calls=%fused_computation.113 | convolution fusion | flops 1078460416 | bytes 19136512 | tf_op jit(solution)/shard_map/dot_general | solution.py:56
  238.6 67.4 %reduce-scatter.5.cloned.1.call-done = f32[128,3072]{1,0:T(8,128)} async-done(((f32[1024,3072]{1,0:T(8,128)}), f32[128,3072]{1,0:T(8,128)}) %reduce-scatter.5.cloned.1.call-update) | async-done | bytes 1572880 | tf_op jit(solution)/shard_map/reduce_scatter | solution.py:294
  308.4 117.6 %reduce-scatter.9.cloned.1.call-done = f32[128,4096]{1,0:T(8,128)} async-done(((f32[1024,4096]{1,0:T(8,128)}), f32[128,4096]{1,0:T(8,128)}) %reduce-scatter.9.cloned.1.call-update) | async-done | bytes 2097168 | tf_op jit(solution)/shard_map/reduce_scatter | solution.py:297
  428.7 117.3 %reduce-scatter.11.cloned.1.call-done = f32[512,1024]{1,0:T(8,128)} async-done(((f32[4096,1024]{1,0:T(8,128)}), f32[512,1024]{1,0:T(8,128)}) %reduce-scatter.11.cloned.1.call-update) | async-done | bytes 2097168 | tf_op jit(solution)/shard_map/reduce_scatter | solution.py:298
  550.6 5.7 fusion.62
  561.5 13.8 %all-reduce.2 = (bf16[1024]{0:T(1024)(128)(2,1)S(1)}, bf16[1024]{0:T(1024)(128)(2,1)S(1)}) all-reduce(f32[1024]{0:T(1024)S(1)} %get-tuple-element.989, f32[1024]{0:T(1024)S(1)} %copy-done.35), channel_id=6, replica_groups=mesh['dp'=4,'sq'=8] {'sq'}, use_global_device_ids=true, to_apply=%region_25.26.clone | all-reduce | flops 2048 | bytes 12288
  575.5 12.4 %all-reduce.3 = (bf16[128]{0:T(256)(128)(2,1)S(1)}, bf16[128]{0:T(256)(128)(2,1)S(1)}) all-reduce(bf16[128]{0:T(256)(128)(2,1)S(1)} %dynamic-slice.7, bf16[128]{0:T(256)(128)(2,1)S(1)} %dynamic-slice.6), channel_id=1, replica_groups=mesh['dp'=4,'sq'=8] {'dp'}, use_global_device_ids=true, to_apply=%region_26.27 | all-reduce | flops 256 | bytes 1024 | tf_op jit(solution)/shard_map/psum | solution.py:301
  590.0 81.7 %all-reduce.7.cloned.1.call-done = (bf16[128,3072]{1,0:T(8,128)(2,1)}, bf16[128,1024]{1,0:T(8,128)(2,1)}, bf16[128,4096]{1,0:T(8,128)(2,1)}, bf16[512,1024]{1,0:T(8,128)(2,1)}) async-done(((bf16[128,3072]{1,0:T(8,128)(2,1)}, bf16[128,1024]{1,0:T(8,128)(2,1)}, bf16[128,4096]{1,0:T(8,128)(2,1)}, bf16[512,1024]{1,0:T(8,128)(2,1)}), (bf16[128,3072]{1,0:T(8,128)(2,1)}, bf16[128,1024]{1,0:T(8,128)(2,1)}, ...) | async-done | bytes 3145744 | tf_op jit(solution)/shard_map/psum | solution.py:302
  (264 shorter events, 163.9 us)
Async XLA Ops:
  7.2 70.4 %copy-start = (bf16[1024,1024]{1,0:T(8,128)(2,1)S(1)}, bf16[1024,1024]{1,0:T(8,128)(2,1)}, u32[]{:S(2)}) copy-start(bf16[1024,1024]{1,0:T(8,128)(2,1)} %param.24) | copy-start | bytes 6291460
  7.2 48.4 %all-gather.9.cloned.1.call-start = ((), (), s32[]{:S(2)}) async-start(), calls=%async_computation.8 | async-start | bytes 2359296 | tf_op jit(solution)/shard_map/all_gather | solution.py:151
  13.9 16.0 %copy-start.11 = (bf16[128,1024]{1,0:T(8,128)(2,1)S(1)}, bf16[128,1024]{1,0:T(8,128)(2,1)}, u32[]{:S(2)}) copy-start(bf16[128,1024]{1,0:T(8,128)(2,1)} %get-tuple-element.1087) | copy-start | bytes 786436
  13.9 91.0 %all-gather.13.cloned.1.call-start = ((), (), s32[]{:S(2)}) async-start(), calls=%async_computation.10 | async-start | bytes 2359296 | tf_op jit(solution)/shard_map/all_gather | solution.py:266
  14.7 119.8 %all-gather.11.cloned.1.call-start = ((), (), s32[]{:S(2)}) async-start(), calls=%async_computation.9 | async-start | bytes 2359296 | tf_op jit(solution)/shard_map/all_gather | solution.py:217
  14.7 7.7 %collective-permute-start = (bf16[1,128,1024]{2,1,0:T(8,128)(2,1)S(1)}, bf16[1,128,1024]{2,1,0:T(8,128)(2,1)}, u32[]{:S(2)}, u32[]{:S(2)}) collective-permute-start(bf16[1,128,1024]{2,1,0:T(8,128)(2,1)S(1)} %get-tuple-element.1086), channel_id=1, source_target_pairs={{0,1},{1,2},{2,3},{3,4},{4,5},{5,6},{6,7},{7,0},{8,9},{9,10},{10,1... | collective-permute-start | bytes 786440 | tf_op jit(solution)/shard_map/ppermute | solution.py:138
  15.2 11.3 %collective-permute-start.1 = (bf16[1,128,1024]{2,1,0:T(8,128)(2,1)S(1)}, bf16[1,128,1024]{2,1,0:T(8,128)(2,1)}, u32[]{:S(2)}, u32[]{:S(2)}) collective-permute-start(bf16[1,128,1024]{2,1,0:T(8,128)(2,1)S(1)} %get-tuple-element.1086), channel_id=1, source_target_pairs={{0,7},{1,0},{2,1},{3,2},{4,3},{5,4},{6,5},{7,6},{8,15},{9,8},{10,9... | collective-permute-start | bytes 786440 | tf_op jit(solution)/shard_map/ppermute | solution.py:143
  18.2 144.4 %all-gather.15.cloned.1.call-start = ((), (), s32[]{:S(2)}) async-start(), calls=%async_computation.11 | async-start | bytes 2359296 | tf_op jit(solution)/shard_map/all_gather | solution.py:267
  22.4 9.8 %collective-permute-start.2 = (bf16[1,128,1024]{2,1,0:T(8,128)(2,1)}, bf16[1,128,1024]{2,1,0:T(8,128)(2,1)}, u32[]{:S(2)}, u32[]{:S(2)}) collective-permute-start(bf16[1,128,1024]{2,1,0:T(8,128)(2,1)} %collective-permute-done), channel_id=1, source_target_pairs={{0,1},{1,2},{2,3},{3,4},{4,5},{5,6},{6,7},{7,0},{8,9},{9,10},{10,1... | collective-permute-start | bytes 786440 | tf_op jit(solution)/shard_map/ppermute | solution.py:138
  26.5 9.1 %collective-permute-start.3 = (bf16[1,128,1024]{2,1,0:T(8,128)(2,1)}, bf16[1,128,1024]{2,1,0:T(8,128)(2,1)S(1)}, u32[]{:S(2)}, u32[]{:S(2)}) collective-permute-start(bf16[1,128,1024]{2,1,0:T(8,128)(2,1)} %collective-permute-done.1), channel_id=1, source_target_pairs={{0,7},{1,0},{2,1},{3,2},{4,3},{5,4},{6,5},{7,6},{8,15},{9,8},{10,9... | collective-permute-start | bytes 786440 | tf_op jit(solution)/shard_map/ppermute | solution.py:143
  32.3 7.7 %collective-permute-start.4 = (bf16[1,128,1024]{2,1,0:T(8,128)(2,1)}, bf16[1,128,1024]{2,1,0:T(8,128)(2,1)S(1)}, u32[]{:S(2)}, u32[]{:S(2)}) collective-permute-start(bf16[1,128,1024]{2,1,0:T(8,128)(2,1)} %collective-permute-done.2), channel_id=1, source_target_pairs={{0,1},{1,2},{2,3},{3,4},{4,5},{5,6},{6,7},{7,0},{8,9},{9,10},{10,1... | collective-permute-start | bytes 786440 | tf_op jit(solution)/shard_map/ppermute | solution.py:138
  35.6 12.0 %collective-permute-start.5 = (bf16[1,128,1024]{2,1,0:T(8,128)(2,1)S(1)}, bf16[1,128,1024]{2,1,0:T(8,128)(2,1)S(1)}, u32[]{:S(2)}, u32[]{:S(2)}) collective-permute-start(bf16[1,128,1024]{2,1,0:T(8,128)(2,1)S(1)} %collective-permute-done.3), channel_id=1, source_target_pairs={{0,7},{1,0},{2,1},{3,2},{4,3},{5,4},{6,5},{7,6},{8,15},{9,8},{10,9... | collective-permute-start | bytes 786440 | tf_op jit(solution)/shard_map/ppermute | solution.py:143
  39.9 11.0 %collective-permute-start.6 = (bf16[1,128,1024]{2,1,0:T(8,128)(2,1)S(1)}, bf16[1,128,1024]{2,1,0:T(8,128)(2,1)S(1)}, u32[]{:S(2)}, u32[]{:S(2)}) collective-permute-start(bf16[1,128,1024]{2,1,0:T(8,128)(2,1)S(1)} %collective-permute-done.4), channel_id=1, source_target_pairs={{0,1},{1,2},{2,3},{3,4},{4,5},{5,6},{6,7},{7,0},{8,9},{9,10},{10,1... | collective-permute-start | bytes 786440 | tf_op jit(solution)/shard_map/ppermute | solution.py:138
  79.2 16.2 %copy-start.33 = (f32[128]{0:T(128)}, f32[128]{0:T(128)S(1)}, u32[]{:S(2)}) copy-start(f32[128]{0:T(128)S(1)} %fusion.88) | copy-start | bytes 1540
  79.2 12.7 %slice-start = ((s8[8388608]{0:T(1024)(128)(4,1)}), s8[4194304]{0:T(1024)(128)(4,1)S(1)}, s32[]{:S(2)}) async-start(s8[8388608]{0:T(1024)(128)(4,1)} %bitcast.213), calls=%async_computation.13 | async-start | bytes 8388608
  98.3 138.6 %reduce-scatter.7.cloned.1.call-start = ((), (), s32[]{:S(2)}) async-start(), calls=%async_computation.5 | async-start | bytes 4718592 | tf_op jit(solution)/shard_map/reduce_scatter | solution.py:295
  102.2 203.8 %reduce-scatter.5.cloned.1.call-start = ((), (), s32[]{:S(2)}) async-start(), calls=%async_computation.4 | async-start | bytes 14155776 | tf_op jit(solution)/shard_map/reduce_scatter | solution.py:294
  167.5 38.2 %copy-start.31 = (f32[1024]{0:T(1024)S(1)}, f32[1024]{0:T(1024)}, u32[]{:S(2)}) copy-start(f32[1024]{0:T(1024)} %param.22) | copy-start | bytes 12292
  167.5 38.2 %copy-start.37 = (f32[128]{0:T(128)S(1)}, f32[128]{0:T(128)}, u32[]{:S(2)}) copy-start(f32[128]{0:T(128)} %copy-done.36) | copy-start | bytes 1540
  213.2 212.7 %reduce-scatter.9.cloned.1.call-start = ((), (), s32[]{:S(2)}) async-start(), calls=%async_computation.6 | async-start | bytes 18874368 | tf_op jit(solution)/shard_map/reduce_scatter | solution.py:297
  225.8 320.2 %reduce-scatter.11.cloned.1.call-start = ((), (), s32[]{:S(2)}) async-start(), calls=%async_computation.7 | async-start | bytes 18874368 | tf_op jit(solution)/shard_map/reduce_scatter | solution.py:298
  236.8 434.9 %all-reduce.7.cloned.1.call-start = ((), (), s32[]{:S(2)}) async-start(), calls=%async_computation.12 | async-start | bytes 6291456 | tf_op jit(solution)/shard_map/psum | solution.py:302
  556.3 32.7 %copy-start.40 = (f32[128]{0:T(128)S(1)}, f32[128]{0:T(128)}, u32[]{:S(2)}) copy-start(f32[128]{0:T(128)} %copy-done.39) | copy-start | bytes 1540
  556.4 32.7 %copy-start.6 = (f32[128,1024]{1,0:T(8,128)S(1)}, f32[128,1024]{1,0:T(8,128)}, u32[]{:S(2)}) copy-start(f32[128,1024]{1,0:T(8,128)} %copy-done.5) | copy-start | bytes 1572868
  (39 other events, 135.8 us)
Sparse Core Ops, SparseCore 0:
  14.1 36.0 all-gather.8
  52.0 27.9 all-gather.12
  82.5 27.9 all-gather.10
  112.2 28.0 all-gather.14
  143.4 51.3 reduce-scatter.6
  213.4 92.6 reduce-scatter.4
  310.0 115.9 reduce-scatter.8
  430.0 115.9 reduce-scatter.10
  549.3 122.2 all-reduce.6
